TPU v7x, 512 devices: a whole 4x4x16 slice. The times are simulated.
512 devices in a mesh: fsdp: 2 (over z_hi), seq: 32 (over x, y, core), tp: 8 (over z_lo).
Axes of the slice: x: 4, y: 4, z: 16 (z_hi: 2, z_lo: 8; z = z_hi * 8 + z_lo), core: 2. Of those that a mesh axis runs over, the one named last changes fastest.
Arguments:
- tokens: bfloat16 [16384, 8192], P(('fsdp', 'seq', 'tp')), may hold values from -6 to 6
- proj_mean: bfloat16 [8192, 4096], P(('fsdp', 'seq'), 'tp'), may hold values from -0.0625 to 0.0625
- proj_devs: bfloat16 [4, 8192, 4096], P(None, ('fsdp', 'seq'), 'tp'), may hold values from -0.0625 to 0.0625
- bc_mean: bfloat16 [8192, 2, 1024], P(('fsdp', 'seq'), None, 'tp'), may hold values from -0.0625 to 0.0625
- bc_devs: bfloat16 [4, 8192, 2, 1024], P(None, ('fsdp', 'seq'), None, 'tp'), may hold values from -0.0625 to 0.0625
- swag_coef: float32 [4], replicated, may hold values from -4 to 4
- dt_weight: bfloat16 [8192, 64], P(('fsdp', 'seq'), 'tp'), may hold values from -0.0625 to 0.0625
- dt_bias: float32 [64], P('tp'), may hold values from -12 to -2, as said below
- decay_rate: float32 [64], P('tp'), may hold values from 0 to 16, as said below
- skip_gain: float32 [64], P('tp'), may hold values from 0.5 to 1.5
- conv_proj: float32 [4, 4096], P(None, 'tp'), may hold values from -3 to 3
- conv_bc: float32 [4, 2, 1024], P(None, None, 'tp'), may hold values from -1.5 to 1.5
Outputs:
- ssm_out: bfloat16 [16384, 4096], P(('fsdp', 'seq'), 'tp')
Inputs may be any that keep to these rules, and one draw needn't show every extreme that they name: `dt_bias`: every bias is the inverse softplus of a positive step size. `decay_rate`: every rate is positive.
All inputs are finite; a program needn't handle non-finite values.
Results may differ from a plain program's by a relative error of at most 0.0059.
Values may be sent and summed in bfloat16 or wider, within the bound.
A program may use at most 64 MiB of HBM per device.

v0:
```python
import jax
import jax.numpy as jnp
from jax import lax
from jax.sharding import PartitionSpec as P

P_SIZE = 64
N = 128
CONV = 4
SPAN = 128


def shifted(shard, axis, by):
    count = lax.axis_size(axis)
    pairs = [(i, i + by) for i in range(count) if 0 <= i + by < count]
    return lax.ppermute(shard, axis, pairs)


def prefix(part, axis, combine, identity):
    place = lax.axis_index(axis)
    gathered = jax.tree.map(lambda a: lax.all_gather(a, axis), part)
    state = jax.tree.map(lambda a, e: jnp.zeros_like(a) + jnp.asarray(e, a.dtype), part, identity)

    def one(hop, state):
        return combine(
            state, jax.tree.map(lambda a: lax.dynamic_index_in_dim(a, hop, 0, False), gathered)
        )

    return lax.fori_loop(0, place, one, state)


def sampled(mean_part, dev_part, swag_coef):
    factor = (2.0 * (dev_part.shape[0] - 1)) ** (-0.5)
    accum = mean_part.astype(jnp.float32)
    for member in range(dev_part.shape[0]):
        accum = accum + factor * swag_coef[member] * dev_part[member].astype(jnp.float32)
    return accum.astype(jnp.bfloat16)


def combine(former, latter):
    return (former[0] * latter[0], latter[0][:, None, None] * former[1] + latter[1])


def body(
    tokens,
    proj_mean,
    proj_devs,
    bc_mean,
    bc_devs,
    swag_coef,
    dt_weight,
    dt_bias,
    decay_rate,
    skip_gain,
    conv_proj,
    conv_bc,
):
    heads_here = decay_rate.shape[0]
    groups_here = bc_mean.shape[2] // N
    width_x = proj_mean.shape[1]
    width_bc = 2 * bc_mean.shape[2]
    rows_all = lax.all_gather(tokens, "tp", axis=0, tiled=True)
    tok_count = rows_all.shape[0]
    weight_x = sampled(proj_mean, proj_devs, swag_coef)
    weight_bc = sampled(bc_mean, bc_devs, swag_coef).reshape(bc_mean.shape[0], width_bc)
    weight_all = jnp.concatenate([weight_x, weight_bc], axis=1)
    projected = jnp.dot(
        rows_all,
        lax.all_gather(weight_all, ("fsdp", "seq"), axis=0, tiled=True),
        preferred_element_type=jnp.float32,
    ).astype(jnp.bfloat16)
    step_size = jax.nn.softplus(
        jnp.dot(
            rows_all,
            lax.all_gather(dt_weight, ("fsdp", "seq"), axis=0, tiled=True),
            preferred_element_type=jnp.float32,
        )
        + dt_bias
    )
    rim_rows = shifted(projected[tok_count - (CONV - 1) :], "seq", 1)
    padded = jnp.concatenate([rim_rows, projected], axis=0).astype(jnp.float32)
    kernel = jnp.concatenate([conv_proj, conv_bc.reshape(CONV, width_bc)], axis=1)
    conv_sum = kernel[0] * padded[0:tok_count]
    for offset in range(1, CONV):
        conv_sum = conv_sum + kernel[offset] * padded[offset : offset + tok_count]
    conved = jax.nn.silu(conv_sum).astype(jnp.bfloat16)
    blocks = tok_count // SPAN
    per_group = heads_here // groups_here
    values = conved[:, :width_x].reshape(blocks, SPAN, heads_here, P_SIZE)
    keys_b = conved[:, width_x : width_x + width_bc // 2].reshape(blocks, SPAN, groups_here, N)
    reads_c = conved[:, width_x + width_bc // 2 :].reshape(blocks, SPAN, groups_here, N)
    steps_b = step_size.reshape(blocks, SPAN, heads_here)
    cum_log = jnp.cumsum(-steps_b * decay_rate, axis=1)
    last_cum = cum_log[:, SPAN - 1 :, :]
    scaled = (
        values.astype(jnp.float32) * (jnp.exp(last_cum - cum_log) * steps_b)[..., None]
    ).astype(jnp.bfloat16)
    keys_h = jnp.repeat(keys_b, per_group, axis=2)
    states = jnp.einsum("bshn,bshp->bhnp", keys_h, scaled, preferred_element_type=jnp.float32)
    block_decay = jnp.exp(last_cum[:, 0, :])
    total_decay = block_decay[0]
    total_state = states[0]
    member = 1
    total_decay, total_state = combine(
        (total_decay, total_state), (block_decay[member], states[member])
    )
    incoming = prefix(
        (total_decay, total_state),
        "seq",
        combine,
        (jnp.ones((heads_here,), jnp.float32), jnp.zeros((heads_here, N, P_SIZE), jnp.float32)),
    )
    scores = jnp.einsum("bqgn,bsgn->bgqs", reads_c, keys_b, preferred_element_type=jnp.float32)
    scores = jnp.repeat(scores, per_group, axis=1)
    causal_mask = jnp.tril(jnp.ones((SPAN, SPAN), bool))
    later_cum = jnp.transpose(cum_log, (0, 2, 1))
    cum_gaps = later_cum[:, :, :, None] - later_cum[:, :, None, :]
    decays = jnp.where(causal_mask, jnp.exp(jnp.minimum(cum_gaps, 0.0)), 0.0)
    weights = (scores * decays * jnp.transpose(steps_b, (0, 2, 1))[:, :, None, :]).astype(
        jnp.bfloat16
    )
    inner_part = jnp.einsum("bhqs,bshp->bqhp", weights, values, preferred_element_type=jnp.float32)
    carried = incoming[1]
    entering = []
    for member in range(blocks):
        entering.append(carried)
        carried = block_decay[member][:, None, None] * carried + states[member]
    entering_bf = jnp.stack(entering).astype(jnp.bfloat16)
    reads_h = jnp.repeat(reads_c, per_group, axis=2)
    outer_part = jnp.exp(cum_log)[..., None] * jnp.einsum(
        "bqhn,bhnp->bqhp", reads_h, entering_bf, preferred_element_type=jnp.float32
    )
    result = inner_part + outer_part + skip_gain[:, None] * values.astype(jnp.float32)
    return result.reshape(tok_count, width_x).astype(jnp.bfloat16)


def solution(mesh):
    return jax.shard_map(
        body,
        mesh=mesh,
        in_specs=(
            P(("fsdp", "seq", "tp"), None),
            P(("fsdp", "seq"), "tp"),
            P(None, ("fsdp", "seq"), "tp"),
            P(("fsdp", "seq"), None, "tp"),
            P(None, ("fsdp", "seq"), None, "tp"),
            P(),
            P(("fsdp", "seq"), "tp"),
            P("tp"),
            P("tp"),
            P("tp"),
            P(None, "tp"),
            P(None, None, "tp"),
        ),
        out_specs=P(("fsdp", "seq"), "tp"),
        check_vma=False,
    )
```

profile of v0, /device:TPU:31, one launch (start us, length us, event | category | flops | bytes accessed | tf_op | source)
XLA Modules:
  0.0 457.1 jit_solution(740776401347183553)
XLA Ops:
  7.3 1.5 fusion.31
  11.3 1.2 fusion.26
  12.5 1.3 fusion.21
  14.6 148.3 %all_gather.19 = bf16[8192,8]{0,1:T(8,128)(2,1)S(1)} all-gather(bf16[128,8]{0,1:T(8,128)(2,1)} %param.20), channel_id=1, replica_groups=mesh['fsdp'=2,'seq'=32,'tp'=8] {'fsdp','seq'}, dimensions={0}, use_global_device_ids=true | all-gather | bytes 133120 | tf_op jit(solution)/shard_map/all_gather | solution.py:74
  164.3 3.4 compare_select_fusion
  168.1 160.6 %all-gather.5.cloned.1.call-done = bf16[8192,768]{1,0:T(8,128)(2,1)} async-done(((bf16[128,768]{1,0:T(8,128)(2,1)}), bf16[8192,768]{1,0:T(8,128)(2,1)}) %all-gather.5.cloned.1.call-update) | async-done | bytes 12582928 | tf_op jit(solution)/shard_map/all_gather | solution.py:68
  328.8 9.3 %fusion.4 = bf16[256,768]{1,0:T(8,128)(2,1)S(1)} fusion(bf16[256,8192]{1,0:T(8,128)(2,1)} %all-gather.7.cloned.1.call-done, bf16[8192,768]{1,0:T(8,128)(2,1)} %all-gather.5.cloned.1.call-done), kind=kOutput, calls=%fused_computation.10 | convolution fusion | flops 3221422080 | bytes 17170432 | tf_op jit(solution)/shard_map/dot_general | solution.py:66
  338.0 1.3 collective-permute-start
  339.4 1.7 collective-permute-done
  343.6 23.8 %all-gather = f32[32,1,8]{2,1,0:T(1,128)S(1)} all-gather(f32[1,1,8]{2,1,0:T(1,128)S(1)} %get-tuple-element.87), channel_id=1, replica_groups=mesh['fsdp'=2,'seq'=32,'tp'=8] {'seq'}, dimensions={0}, use_global_device_ids=true | all-gather | bytes 1056 | tf_op jit(solution)/shard_map/all_gather | solution.py:20
  367.6 37.6 %all-gather.9.cloned.1.call-done = f32[32,8,128,64]{2,3,1,0:T(8,128)} async-done(((f32[1,8,128,64]{2,3,1,0:T(8,128)}), f32[32,8,128,64]{2,3,1,0:T(8,128)}) %all-gather.9.cloned.1.call-update) | async-done | bytes 8388624 | tf_op jit(solution)/shard_map/all_gather | solution.py:20
  405.2 42.7 %while.12 = (s32[]{:T(128)}, f32[8,128,64]{2,1,0:T(8,128)S(1)}, s32[]{:T(128)}, f32[32,8]{1,0:T(8,128)S(1)}, f32[32,8,128,64]{2,3,1,0:T(8,128)}, /*index=5*/s32[]{:T(128)}, s32[]{:T(128)}, s32[]{:T(128)}) while((s32[]{:T(128)}, f32[8,128,64]{2,1,0:T(8,128)S(1)}, s32[]{:T(128)}, f32[32,8]{1,0:T(8,128)S(1)}, f32[32,8,128,64]{2,3,1,0:T(8,128)}, ...), condition=%wide.region_2.3_spmd, body=%wide.region_1.2_spmd.sunk | while | flops 131077 | bytes 1835231 | solution.py:28
  405.2 1.0 constant_dynamic-slice_fusion.2
  406.6 1.0 constant_dynamic-slice_fusion.2
  408.0 1.0 constant_dynamic-slice_fusion.2
  412.1 1.0 constant_dynamic-slice_fusion.2
  413.5 1.0 constant_dynamic-slice_fusion.2
  414.9 1.0 constant_dynamic-slice_fusion.2
  416.2 1.0 constant_dynamic-slice_fusion.2
  417.6 1.0 constant_dynamic-slice_fusion.2
  424.5 1.0 constant_dynamic-slice_fusion.2
  425.9 1.0 constant_dynamic-slice_fusion.2
  427.3 1.0 constant_dynamic-slice_fusion.2
  428.6 1.0 constant_dynamic-slice_fusion.2
  430.0 1.0 constant_dynamic-slice_fusion.2
  431.4 1.0 constant_dynamic-slice_fusion.2
  438.3 1.0 constant_dynamic-slice_fusion.2
  439.6 1.0 constant_dynamic-slice_fusion.2
  441.0 1.0 constant_dynamic-slice_fusion.2
  442.4 1.0 constant_dynamic-slice_fusion.2
  443.8 1.0 constant_dynamic-slice_fusion.2
  449.6 1.0 reshape.103
  (148 shorter events, 30.4 us)
Async XLA Ops:
  6.5 161.3 %copy-start = (f32[8]{0:T(128)S(1)}, f32[8]{0:T(128)}, u32[]{:S(2)}) copy-start(f32[8]{0:T(128)} %param.22) | copy-start | bytes 100
  6.5 157.7 %all-gather.7.cloned.1.call-start = ((), (), s32[]{:S(2)}) async-start(), calls=%async_computation.1 | async-start | bytes 4718592 | tf_op jit(solution)/shard_map/all_gather | solution.py:61
  7.3 321.5 %all-gather.5.cloned.1.call-start = ((), (), s32[]{:S(2)}) async-start(), calls=%async_computation | async-start | bytes 12779520 | tf_op jit(solution)/shard_map/all_gather | solution.py:68
  14.5 390.6 %all-gather.9.cloned.1.call-start = ((), (), s32[]{:S(2)}) async-start(), calls=%async_computation.2 | async-start | bytes 8650752 | tf_op jit(solution)/shard_map/all_gather | solution.py:20
  338.0 3.1 collective-permute-start
  405.2 43.5 %copy-start.1 = (f32[8]{0:T(128)S(1)}, f32[8]{0:T(128)}, u32[]{:S(2)}) copy-start(f32[8]{0:T(128)} %param.23) | copy-start | bytes 100
Sparse Core Ops, SparseCore 0:
  9.4 109.3 all-gather.6
  123.3 205.4 all-gather.4
  343.6 61.5 all-gather.8
where the time goes:
time: 458 us; the launch traced here: 457 us
  waiting for transfers between devices  201 us (44%)
  blocking collectives  172 us (38%)
  local copies, waits for them, and re-layouts  42.2 us (9%)
  between operations  15.8 us (3%)
  matrix products  14.1 us (3%)
  other arithmetic  9.38 us (2%)
    all_gather x1, waiting for transfers between devices, body(): lax.all_gather(weight_all, ('fsdp', 'seq'), axis=0, tiled=True)  161 us
    all_gather x1, blocking collectives, body(): lax.all_gather(dt_weight, ('fsdp', 'seq'), axis=0, tiled=True)  148 us
    all_gather x1, waiting for transfers between devices, prefix(): gathered = jax.tree.map(lambda a: lax.all_gather(a, axis), part)  37.6 us
    dynamic_slice x62, local copies, waits for them, and re-layouts, one(): lax.dynamic_index_in_dim(a, hop, 0, False)  36.4 us
    all_gather x1, blocking collectives, prefix(): gathered = jax.tree.map(lambda a: lax.all_gather(a, axis), part)  23.8 us
    dot_general x1, matrix products, body(): jnp.dot(rows_all, lax.all_gather(weight_all, ('fsdp', 'seq'), axis=0, til...  9.25 us
  transfers between devices with their start and end apart: 4, of which 3 were waited for; matrix products, arithmetic and copies ran while one was open for 2% of the time, Pallas kernels for 0%

commit v1 on v0

--- a/solution.py
+++ b/solution.py
@@ -63,10 +63,14 @@
     weight_x = sampled(proj_mean, proj_devs, swag_coef)
     weight_bc = sampled(bc_mean, bc_devs, swag_coef).reshape(bc_mean.shape[0], width_bc)
     weight_all = jnp.concatenate([weight_x, weight_bc], axis=1)
+
+    def push_lines(incoming_x):
+        res = tuple((incoming_x for _ in range(lax.axis_size(("fsdp", "seq")))))
+        then = jnp.stack(res)
+        return jnp.concatenate(lax.all_to_all(then, ("fsdp", "seq"), 0, 0), axis=0)
+
     projected = jnp.dot(
-        rows_all,
-        lax.all_gather(weight_all, ("fsdp", "seq"), axis=0, tiled=True),
-        preferred_element_type=jnp.float32,
+        rows_all, push_lines(weight_all), preferred_element_type=jnp.float32
     ).astype(jnp.bfloat16)
     step_size = jax.nn.softplus(
         jnp.dot(

time: 458 us -> 942 us (2.06)
  blocking collectives: 172 us -> 758 us
  waiting for transfers between devices: 201 us -> 71.9 us
  starting transfers between devices: 1.38 us -> 23 us
    all_gather x1, blocking collectives: 148 us -> 739 us  [body(): lax.all_gather(dt_weight, ('fsdp', 'seq'), axis=0, tiled=True)]
    all_gather x1 -> x0, waiting for transfers between devices: 161 us -> none  [body(): lax.all_gather(weight_all, ('fsdp', 'seq'), axis=0, tiled=True)]
    all_gather x1, waiting for transfers between devices: 37.6 us -> 69.5 us  [prefix(): gathered = jax.tree.map(lambda a: lax.all_gather(a, axis), part)]
    all_to_all x0 -> x1, starting transfers between devices: none -> 21.6 us  [push_lines(): return jnp.concatenate(lax.all_to_all(then, ('fsdp', 'seq'), 0, 0), axis=0)]
  transfers between devices with their start and end apart: 4 -> 4, of which waited for: 3 -> 2; matrix products, arithmetic and copies ran while one was open for 2% -> 0% of each run, Pallas kernels for 0% -> 0%
where the time goes in v1:
time: 942 us; the launch traced here: 941 us
  blocking collectives  758 us (80%)
  waiting for transfers between devices  71.9 us (8%)
  local copies, waits for them, and re-layouts  46.8 us (5%)
  starting transfers between devices  23 us (2%)
  between operations  16.2 us (2%)
  matrix products  14.1 us (1%)
    all_gather x1, blocking collectives, body(): lax.all_gather(dt_weight, ('fsdp', 'seq'), axis=0, tiled=True)  739 us
    all_gather x1, waiting for transfers between devices, prefix(): gathered = jax.tree.map(lambda a: lax.all_gather(a, axis), part)  69.5 us
    dynamic_slice x62, local copies, waits for them, and re-layouts, one(): lax.dynamic_index_in_dim(a, hop, 0, False)  36.4 us
    all_to_all x1, starting transfers between devices, push_lines(): return jnp.concatenate(lax.all_to_all(then, ('fsdp', 'seq'), 0, 0), axis=0)  21.6 us
    all_gather x1, blocking collectives, prefix(): gathered = jax.tree.map(lambda a: lax.all_gather(a, axis), part)  19 us
  transfers between devices with their start and end apart: 4, of which 2 were waited for; matrix products, arithmetic and copies ran while one was open for 0% of the time, Pallas kernels for 0%

profile of v1, /device:TPU:31, one launch (start us, length us, event | category | flops | bytes accessed | tf_op | source)
XLA Modules:
  0.0 940.6 jit_solution(9102103460210869190)
XLA Ops:
  6.5 1.5 fusion.31
  10.5 1.2 fusion.26
  11.7 1.3 fusion.21
  13.1 6.0 stack.11
  19.1 21.6 %all-to-all-start = ((bf16[64,128,768]{2,1,0:T(8,128)(2,1)}), bf16[64,128,768]{2,1,0:T(8,128)(2,1)}, u32[]{:S(2)}, u32[]{:S(2)}) async-start(bf16[64,128,768]{2,1,0:T(8,128)(2,1)} %stack.11), calls=%async_computation | async-start | bytes 25165824 | tf_op jit(solution)/shard_map/all_to_all | solution.py:70
  41.5 739.3 %all_gather.15 = bf16[8192,8]{0,1:T(8,128)(2,1)S(1)} all-gather(bf16[128,8]{0,1:T(8,128)(2,1)S(1)} %copy-done.2), channel_id=1, replica_groups=mesh['fsdp'=2,'seq'=32,'tp'=8] {'fsdp','seq'}, dimensions={0}, use_global_device_ids=true | all-gather | bytes 133120 | tf_op jit(solution)/shard_map/all_gather | solution.py:78
  780.9 3.4 compare_select_fusion
  784.7 9.3 fusion.4
  794.0 1.3 collective-permute-start
  795.4 1.7 collective-permute-done
  799.6 19.0 %all-gather = f32[32,1,8]{2,1,0:T(1,128)S(1)} all-gather(f32[1,1,8]{2,1,0:T(1,128)S(1)} %get-tuple-element.87), channel_id=1, replica_groups=mesh['fsdp'=2,'seq'=32,'tp'=8] {'seq'}, dimensions={0}, use_global_device_ids=true | all-gather | bytes 1056 | tf_op jit(solution)/shard_map/all_gather | solution.py:20
  818.8 69.5 %all-gather.6.cloned.1.call-done = f32[32,8,128,64]{2,3,1,0:T(8,128)} async-done(((f32[1,8,128,64]{2,3,1,0:T(8,128)}), f32[32,8,128,64]{2,3,1,0:T(8,128)}) %all-gather.6.cloned.1.call-update) | async-done | bytes 8388624 | tf_op jit(solution)/shard_map/all_gather | solution.py:20
  888.4 42.7 %while.12 = (s32[]{:T(128)}, f32[8,128,64]{2,1,0:T(8,128)S(1)}, s32[]{:T(128)}, f32[32,8]{1,0:T(8,128)S(1)}, f32[32,8,128,64]{2,3,1,0:T(8,128)}, /*index=5*/s32[]{:T(128)}, s32[]{:T(128)}, s32[]{:T(128)}) while((s32[]{:T(128)}, f32[8,128,64]{2,1,0:T(8,128)S(1)}, s32[]{:T(128)}, f32[32,8]{1,0:T(8,128)S(1)}, f32[32,8,128,64]{2,3,1,0:T(8,128)}, ...), condition=%wide.region_2.3_spmd, body=%wide.region_1.2_spmd.sunk | while | flops 131077 | bytes 1835231 | solution.py:28
  888.4 1.0 constant_dynamic-slice_fusion.2
  889.8 1.0 constant_dynamic-slice_fusion.2
  891.1 1.0 constant_dynamic-slice_fusion.2
  895.3 1.0 constant_dynamic-slice_fusion.2
  896.6 1.0 constant_dynamic-slice_fusion.2
  898.0 1.0 constant_dynamic-slice_fusion.2
  902.1 1.0 constant_dynamic-slice_fusion.2
  903.5 1.0 constant_dynamic-slice_fusion.2
  904.9 1.0 constant_dynamic-slice_fusion.2
  909.0 1.0 constant_dynamic-slice_fusion.2
  910.4 1.0 constant_dynamic-slice_fusion.2
  914.5 1.0 constant_dynamic-slice_fusion.2
  915.9 1.0 constant_dynamic-slice_fusion.2
  917.3 1.0 constant_dynamic-slice_fusion.2
  921.4 1.0 constant_dynamic-slice_fusion.2
  922.8 1.0 constant_dynamic-slice_fusion.2
  924.2 1.0 constant_dynamic-slice_fusion.2
  928.3 1.0 constant_dynamic-slice_fusion.2
  932.7 1.0 reshape.109
  (156 shorter events, 29.3 us)
Async XLA Ops:
  19.1 22.4 %copy-start.2 = (bf16[128,8]{0,1:T(8,128)(2,1)S(1)}, bf16[128,8]{0,1:T(8,128)(2,1)}, u32[]{:S(2)}) copy-start(bf16[128,8]{0,1:T(8,128)(2,1)} %param.20) | copy-start | bytes 6148
  19.1 761.7 %copy-start = (f32[4,512]{1,0:T(4,128)S(1)}, f32[4,512]{1,0:T(4,128)}, u32[]{:S(2)}) copy-start(f32[4,512]{1,0:T(4,128)} %param.24) | copy-start | bytes 24580
  19.1 761.7 %copy-start.1 = (f32[4,2,128]{2,1,0:T(2,128)S(1)}, f32[4,2,128]{2,1,0:T(2,128)}, u32[]{:S(2)}) copy-start(f32[4,2,128]{2,1,0:T(2,128)} %param.25) | copy-start | bytes 12292
  19.1 761.8 %copy-start.3 = (f32[8]{0:T(128)S(1)}, f32[8]{0:T(128)}, u32[]{:S(2)}) copy-start(f32[8]{0:T(128)} %param.21) | copy-start | bytes 100
  19.1 765.4 %copy-start.4 = (f32[8]{0:T(128)S(1)}, f32[8]{0:T(128)}, u32[]{:S(2)}) copy-start(f32[8]{0:T(128)} %param.22) | copy-start | bytes 100
  19.1 765.6 %all-to-all-start = ((bf16[64,128,768]{2,1,0:T(8,128)(2,1)}), bf16[64,128,768]{2,1,0:T(8,128)(2,1)}, u32[]{:S(2)}, u32[]{:S(2)}) async-start(bf16[64,128,768]{2,1,0:T(8,128)(2,1)} %stack.11), calls=%async_computation | async-start | bytes 25165824 | tf_op jit(solution)/shard_map/all_to_all | solution.py:70
  40.7 740.2 %all-gather.4.cloned.1.call-start = ((), (), s32[]{:S(2)}) async-start(), calls=%async_computation.1 | async-start | bytes 4718592 | tf_op jit(solution)/shard_map/all_gather | solution.py:61
  41.4 846.9 %all-gather.6.cloned.1.call-start = ((), (), s32[]{:S(2)}) async-start(), calls=%async_computation.2 | async-start | bytes 8650752 | tf_op jit(solution)/shard_map/all_gather | solution.py:20
  794.0 3.1 collective-permute-start
  888.3 43.4 %copy-start.5 = (f32[8]{0:T(128)S(1)}, f32[8]{0:T(128)}, u32[]{:S(2)}) copy-start(f32[8]{0:T(128)} %param.23) | copy-start | bytes 100
Sparse Core Ops, SparseCore 0:
  43.6 302.9 all-gather.3
  799.5 88.7 all-gather.5
